TPU v7x, 32 devices: a whole 2x2x4 slice. The times are simulated.
32 devices in a mesh: groups: 2 (over x), col: 16 (over z, y, core).
Axes of the slice: x: 2, y: 2, z: 4, core: 2. Of those that a mesh axis runs over, the one named last changes fastest.
Arguments:
- coords: bfloat16 [3, 131072], P(None, ('groups', 'col')), parts along dimension 1, may hold values from 0 to 8
- probes: bfloat16 [64, 131072], P(None, ('groups', 'col')), parts along dimension 1, may hold values from -6 to 6
- order: int32 [131072], P(('groups', 'col')), parts along dimension 0, may hold values from 0 to 65535, as said below
- near_list: int32 [512, 27], P(('groups', 'col')), parts along dimension 0, may hold values from -16 to 271, as said below
- near_count: int32 [512], P(('groups', 'col')), parts along dimension 0, may hold values from 1 to 27
- leaf_basis: bfloat16 [512, 64, 256], P(('groups', 'col')), parts along dimension 0, may hold values from -0.375 to 0.375
- transfer_low: bfloat16 [512, 64, 64], P(('groups', 'col')), parts along dimension 0, may hold values from -0.5 to 0.5
- transfer_top: bfloat16 [256, 64, 64], P(('groups', 'col')), parts along dimension 0, may hold values from -0.5 to 0.5
- coupling_leaf: bfloat16 [512, 16, 64, 64], P(('groups', 'col')), parts along dimension 0, may hold values from -0.1875 to 0.1875
- coupling_mid: bfloat16 [256, 16, 64, 64], P(('groups', 'col')), parts along dimension 0, may hold values from -0.1875 to 0.1875
- coupling_top: bfloat16 [128, 16, 64, 64], P(('groups', 'col')), parts along dimension 0, may hold values from -0.1875 to 0.1875
- far_leaf: int32 [512, 16], P(('groups', 'col')), parts along dimension 0, may hold values from -16 to 271, as said below
- far_mid: int32 [256, 16], P(('groups', 'col')), parts along dimension 0, may hold values from -8 to 135, as said below
- far_top: int32 [128, 16], P(('groups', 'col')), parts along dimension 0, may hold values from 0 to 63, as said below
Outputs:
- kernel_product: float32 [64, 131072], P(None, ('groups', 'col')), parts along dimension 1
There are 2 independent parts, one for each index of `groups`. A program takes and returns all parts, laid end to end along the dimension named above; each array names one. Nothing has to cross between parts.
Inputs may be any that keep to these rules, and one draw needn't show every extreme that they name: `order`: each aligned block of 4096 entries is a permutation of that block's own positions. `near_list`: slot 0 of leaf i names i itself; every entry lies within 16 of its leaf's index. `far_leaf`: every entry lies within 16 of its cluster's index. `far_mid`: every entry lies within 8 of its cluster's index. `far_top`: in each aligned block of 4 rows, the entries name at most one cluster of each aligned range of 4 top-level clusters.
All inputs are finite; a program needn't handle non-finite values.
Results may differ from a plain program's by a relative error of at most 0.0034.
The roundings to bfloat16 on the way count: a program that leaves them out, or rounds other values in their place, can miss the bound.
Values may be sent and summed in bfloat16 or wider, within the bound.
A program may use at most 128 MiB of HBM per device.

v0:
```python
import jax
import jax.numpy as jnp
from jax import lax
from jax.experimental import pallas as pl
from jax.experimental.pallas import tpu as pltpu
from jax.sharding import PartitionSpec as P

LEAF = 256
AMPLITUDE = 0.125
LENGTH_SCALE = 1.0
GROUP = 16
CHUNKS = 4
FEATURES = 48
BF16 = jnp.bfloat16
F32 = jnp.float32
MESH = pl.DeviceIdType.MESH
VMEM_BYTES = 60 * 2**20
NT = (((1,), (1,)), ((), ()))


def dot(a, b):
    return jnp.dot(a, b, preferred_element_type=F32)


def dot_nt(a, b):
    return lax.dot_general(a, b, NT, preferred_element_type=F32)


def within(position, points):
    if points & (points - 1) == 0:
        return position & (points - 1)
    return lax.rem(position, points)


def prep_kernel(
    order, near_count, coords, probes, near_list, basis_hbm, low_hbm, top_hbm,
    points_out, cells_out, coef_out, counts_out,
    left, right, cells_left, cells_right, coef_left, coef_right, tops,
    rows_in, rows_out, basis, low, top,
    load_sems, send_sems, recv_sems, top_send, top_recv, pair_send, pair_recv,
):
    points = coords.shape[1]
    probe_rows = probes.shape[0]
    leaves = basis.shape[0]
    spans = lax.axis_size("col")
    device = lax.axis_index("col")
    chips = spans // 2
    chip, side = device // 2, device % 2

    barrier = pltpu.get_barrier_semaphore()

    def greet(to):
        pl.semaphore_signal(barrier, inc=1, device_id={"col": to}, device_id_type=MESH)

    @pl.loop(1, chips)
    def _(j):
        greet(((chip + j) % chips) * 2 + side)

    greet(chip * 2 + 1 - side)
    outer = jnp.where(side == 0, device - 1, device + 1)
    has_outer = (outer >= 0) & (outer < spans)

    @pl.when(has_outer)
    def _():
        greet(outer)

    loads = [
        pltpu.make_async_copy(basis_hbm, basis, load_sems.at[0]),
        pltpu.make_async_copy(low_hbm, low, load_sems.at[1]),
        pltpu.make_async_copy(top_hbm, top, load_sems.at[2]),
    ]
    for load in loads:
        load.start()

    for c in range(points // 256):
        at = slice(c * 256, c * 256 + 256)
        block = jnp.concatenate(
            [
                probes[:, at].astype(F32),
                coords[:, at].astype(F32),
                jnp.zeros((125 - probe_rows, 256), F32),
            ],
            axis=0,
        )
        rows_in[at, :] = block.T

    def put(source, target, k, to):
        return pltpu.make_async_remote_copy(
            src_ref=source,
            dst_ref=target,
            send_sem=send_sems.at[k],
            recv_sem=recv_sems.at[k],
            device_id={"col": to},
            device_id_type=MESH,
        )

    ahead, behind = jnp.minimum(device + 1, spans - 1), jnp.maximum(device - 1, 0)
    is_first, is_last = device == 0, device == spans - 1
    width = points // CHUNKS
    parts = [slice(c * width, c * width + width) for c in range(CHUNKS)]
    to_ahead = [put(points_out.at[:, p], left.at[:, p], c, ahead) for c, p in enumerate(parts)]
    to_ahead.append(put(cells_out, cells_left, CHUNKS, ahead))
    to_ahead.append(put(coef_out, coef_left, CHUNKS + 1, ahead))
    base_sem = CHUNKS + 2
    to_behind = [
        put(points_out.at[:, p], right.at[:, p], base_sem + c, behind) for c, p in enumerate(parts)
    ]
    to_behind.append(put(cells_out, cells_right, base_sem + CHUNKS, behind))
    to_behind.append(put(coef_out, coef_right, base_sem + CHUNKS + 1, behind))

    def launch(c):
        @pl.when(jnp.logical_not(is_last))
        def _():
            to_ahead[c].start()

        @pl.when(jnp.logical_not(is_first))
        def _():
            to_behind[c].start()

    cells = []
    for c in range(CHUNKS):

        @pl.loop(0, width // 16)
        def _(k, c=c):
            base = pl.multiple_of(c * width + k * 16, 16)
            for u in range(16):
                rows_out[pl.ds(base + u, 1), :] = rows_in[
                    pl.ds(within(order[base + u], points), 1), :
                ]

        for d in range(width // LEAF):
            at = slice(c * width + d * LEAF, c * width + d * LEAF + LEAF)
            turned = rows_out[at, :].T
            points_out[:, at] = turned[:probe_rows].astype(BF16)
            cells.append(turned[probe_rows : probe_rows + 4])
        if c == 0:
            pl.semaphore_wait(barrier, chips + jnp.where(has_outer, 1, 0))
        launch(c)

    columns = leaves // 4
    for j in range(columns):
        cells_out[:, j * LEAF : (j + 1) * LEAF] = jnp.concatenate(
            [cells[g * columns + j] for g in range(4)], axis=0
        ).astype(BF16)
    launch(CHUNKS)

    for load in loads:
        load.wait()

    leaf_coef = [
        dot_nt(points_out[:probe_rows, i * LEAF : (i + 1) * LEAF], basis[i]).astype(BF16)
        for i in range(leaves)
    ]
    mid_coef = [
        (dot(leaf_coef[2 * m], low[2 * m]) + dot(leaf_coef[2 * m + 1], low[2 * m + 1])).astype(BF16)
        for m in range(leaves // 2)
    ]
    top_coef = [
        (dot(mid_coef[2 * q], top[2 * q]) + dot(mid_coef[2 * q + 1], top[2 * q + 1])).astype(BF16)
        for q in range(leaves // 4)
    ]
    nodes = leaf_coef + mid_coef
    for m in range(len(nodes) // 2):
        coef_out[m] = jnp.concatenate([nodes[2 * m], nodes[2 * m + 1]], axis=1)
    for q in range(leaves // 8):
        tops[side, chip, q] = jnp.concatenate([top_coef[2 * q], top_coef[2 * q + 1]], axis=1)

    def spread_top(j):
        return pltpu.make_async_remote_copy(
            src_ref=tops.at[side, chip],
            dst_ref=tops.at[side, chip],
            send_sem=top_send.at[j],
            recv_sem=top_recv.at[j],
            device_id={"col": ((chip + j) % chips) * 2 + side},
            device_id_type=MESH,
        )

    @pl.loop(1, chips)
    def _(j):
        spread_top(j).start()

    launch(CHUNKS + 1)

    lane = lax.broadcasted_iota(jnp.int32, (leaves, 128), 1)
    row = lax.broadcasted_iota(jnp.int32, (leaves, 128), 0)
    live = jnp.zeros((leaves, 128), jnp.int32)
    for i in range(leaves):
        live = jnp.where(row == i, near_count[i], live)
    start = device * leaves - leaves
    total = jnp.zeros((leaves, 128), jnp.int32)
    for k in range(near_list.shape[1]):
        named = near_list[:, k : k + 1] - start
        total = total + jnp.where((named == lane) & (live > k), 1, 0)
    inside = (lane + start >= 0) & (lane + start < spans * leaves)
    counts_out[...] = jnp.where(inside, total, 0)

    @pl.loop(1, chips)
    def _(j):
        spread_top(j).wait()

    pair = pltpu.make_async_remote_copy(
        src_ref=tops.at[side],
        dst_ref=tops.at[side],
        send_sem=pair_send,
        recv_sem=pair_recv,
        device_id={"col": chip * 2 + 1 - side},
        device_id_type=MESH,
    )
    pair.start()

    @pl.when(jnp.logical_not(is_last))
    def _():
        for c in range(CHUNKS + 2):
            to_ahead[c].wait_send()
            to_behind[c].wait_recv()

    @pl.when(jnp.logical_not(is_first))
    def _():
        for c in range(CHUNKS + 2):
            to_behind[c].wait_send()
            to_ahead[c].wait_recv()

    pair.wait()


def target_features(cells):
    squares = cells * cells
    high = squares.astype(BF16).astype(F32)
    ones = jnp.ones_like(cells)
    return jnp.concatenate([cells, high, squares - high, ones, ones, jnp.zeros_like(cells)], axis=0)


def source_features(cells):
    squares = cells * cells
    high = squares.astype(BF16).astype(F32)
    ones = jnp.ones_like(cells)
    return jnp.concatenate(
        [-2.0 * cells, ones, ones, high, squares - high, jnp.zeros_like(cells)], axis=0
    )


def leaf_cells(packed, i):
    columns = packed.shape[1] // LEAF
    g, j = i // columns, i % columns
    cells = packed[:, j * LEAF : (j + 1) * LEAF].astype(F32)[4 * g : 4 * g + 4]
    return jnp.concatenate([cells, jnp.zeros_like(cells)], axis=0)


def fill_targets(packed, targets):
    for i in range(targets.shape[0]):
        targets[i] = target_features(leaf_cells(packed, i)).astype(BF16)


def fill_sources(points, packed, sources, values, place):
    for i in range(points.shape[1] // LEAF):
        sources[place + i] = source_features(leaf_cells(packed, i)).T.astype(BF16)
        values[place + i] = points[:, i * LEAF : (i + 1) * LEAF]


def list_pairs(counts, listed, leaves):
    def one(i, position):
        for j in range(2 * leaves + 1):
            count = counts[i, i + j]
            listed[position] = count * 4096 + (i * 64 + i + j)
            position = position + jnp.minimum(count, 1)
        return position

    position = lax.fori_loop(0, leaves, one, jnp.int32(0))
    for u in range(GROUP):
        listed[position + u] = jnp.int32(leaves)
    return (position + (GROUP - 1)) // GROUP


def add_pairs(listed, groups, targets, sources, values, field):
    @pl.loop(0, groups)
    def _(g):
        pairs = [listed[g * GROUP + u] for u in range(GROUP)]
        slots = [pair & 63 for pair in pairs]
        owners = [(pair >> 6) & 63 for pair in pairs]
        weights = [(pair >> 12).astype(F32) * AMPLITUDE for pair in pairs]
        tiles = []
        for u in range(GROUP):
            squared = jnp.maximum(dot(sources[slots[u]], targets[owners[u]]), 1e-30)
            distance = squared * lax.rsqrt(squared)
            tiles.append(jnp.exp(distance * (-1.0 / LENGTH_SCALE)).astype(BF16))
        sums = [dot(values[slots[u]], tiles[u]) * weights[u] for u in range(GROUP)]
        for u in range(GROUP):
            field[owners[u]] += sums[u]


def apply_kernel(
    counts, order, far_leaf, far_mid, far_top,
    own, left, right, cells_own, cells_left, cells_right,
    coef_own, coef_left, coef_right, tops,
    basis, low, top, couple_leaf_hbm, couple_mid_hbm, couple_top_hbm,
    out,
    targets, sources, values, listed, field,
    around_leaf, around_mid, around_top, couple_leaf, couple_mid, couple_top,
    couple_sum, rows_in, rows_out, sems,
):
    leaves = basis.shape[0]
    points = own.shape[1]
    device = lax.axis_index("col")
    spans = lax.axis_size("col")
    copies = [
        pltpu.make_async_copy(couple_top_hbm, couple_top, sems.at[0]),
        pltpu.make_async_copy(couple_mid_hbm, couple_mid, sems.at[1]),
        pltpu.make_async_copy(couple_leaf_hbm, couple_leaf, sems.at[2]),
    ]
    for copy in copies:
        copy.start()

    fill_targets(cells_own, targets)
    fill_sources(left, cells_left, sources, values, 0)
    fill_sources(own, cells_own, sources, values, leaves)
    fill_sources(right, cells_right, sources, values, 2 * leaves)
    field[...] = jnp.zeros_like(field)
    groups = list_pairs(counts, listed, leaves)
    add_pairs(listed, groups, targets, sources, values, field)

    def spread(pair, around, slot):
        one, two = pair[:, :64], pair[:, 64:]
        around[slot] = jnp.concatenate([one, one], axis=1)
        around[slot + 1] = jnp.concatenate([two, two], axis=1)

    mids, quads = leaves // 2, leaves // 4

    def spread_part(coefs, part):
        for m in range(leaves // 2):
            spread(coefs[m], around_leaf, part * leaves + 2 * m)
        for m in range(mids // 2):
            spread(coefs[leaves // 2 + m], around_mid, part * mids + 2 * m)

    spread_part(coef_own, 1)
    for coefs, part, missing in (
        (coef_left, 0, device == 0),
        (coef_right, 2, device == spans - 1),
    ):

        @pl.when(missing)
        def _(part=part):
            at_leaf, at_mid = pl.ds(part * leaves, leaves), pl.ds(part * mids, mids)
            around_leaf[at_leaf] = jnp.zeros((leaves, 64, 128), BF16)
            around_mid[at_mid] = jnp.zeros((mids, 64, 128), BF16)

        @pl.when(jnp.logical_not(missing))
        def _(coefs=coefs, part=part):
            spread_part(coefs, part)

    @pl.loop(0, tops.shape[1])
    def _(chip):
        for side in range(2):
            for q in range(quads // 2):
                spread(tops[side, chip, q], around_top, (2 * chip + side) * quads + 2 * q)

    for copy in copies:
        copy.wait()

    lower_half = lax.broadcasted_iota(jnp.int32, (64, 128), 1) < 64

    def couple(lists, around, matrices, base, place):
        far = lists.shape[1]

        @pl.loop(0, lists.shape[0] // 4)
        def _(block):
            totals = []
            for d in range(4):
                n = block * 4 + d
                total = None
                for f in range(0, far, 4):
                    picked = [around[lists[n, f + e] - base] for e in range(4)]
                    rows = jnp.concatenate(
                        [
                            jnp.where(lower_half, picked[0], picked[1]),
                            jnp.where(lower_half, picked[2], picked[3]),
                        ],
                        axis=1,
                    )
                    term = dot(rows, matrices[n, f : f + 4].reshape(256, 64))
                    total = term if total is None else total + term
                totals.append(total)
            for d in range(4):
                couple_sum[place + block * 4 + d] = totals[d]

    couple(far_top, around_top, couple_top, 0, leaves + mids)
    couple(far_mid, around_mid, couple_mid, device * mids - mids, leaves)
    couple(far_leaf, around_leaf, couple_leaf, device * leaves - leaves, 0)

    upper = [couple_sum[leaves + mids + q].astype(BF16) for q in range(quads)]
    middle = [
        (couple_sum[leaves + m] + dot_nt(upper[m // 2], top[m])).astype(BF16) for m in range(mids)
    ]
    bottom = [
        (couple_sum[i] + dot_nt(middle[i // 2], low[i])).astype(BF16) for i in range(leaves)
    ]
    for i in range(leaves):
        total = field[i] + dot(bottom[i], basis[i])
        rows_in[i * LEAF : (i + 1) * LEAF, :] = jnp.concatenate(
            [total, jnp.zeros_like(total)], axis=0
        ).T

    @pl.loop(0, points // 16)
    def _(k):
        base = pl.multiple_of(k * 16, 16)
        for u in range(16):
            rows_out[pl.ds(within(order[base + u], points), 1), :] = rows_in[pl.ds(base + u, 1), :]

    for c in range(points // 256):
        at = slice(c * 256, c * 256 + 256)
        out[:, at] = rows_out[at, :].T[:64, :]


def vmem():
    return pl.BlockSpec(memory_space=pltpu.VMEM)


def smem():
    return pl.BlockSpec(memory_space=pltpu.SMEM)


def hbm():
    return pl.BlockSpec(memory_space=pl.ANY)


def per_device(
    coords, probes, order, near_list, near_count, leaf_basis, transfer_low, transfer_top,
    coupling_leaf, coupling_mid, coupling_top, far_leaf, far_mid, far_top,
):
    points = coords.shape[1]
    leaves = leaf_basis.shape[0]
    mids, tops = leaves // 2, leaves // 4
    count = lax.axis_size("col")
    chips = count // 2
    shape = jax.ShapeDtypeStruct
    shared = (leaves + mids) // 2
    dma = pltpu.SemaphoreType.DMA

    exchanged = pl.pallas_call(
        prep_kernel,
        out_shape=(
            shape((64, points), BF16),
            shape((16, points // 4), BF16),
            shape((shared, 64, 128), BF16),
            shape((leaves, 128), jnp.int32),
            shape((64, points), BF16),
            shape((64, points), BF16),
            shape((16, points // 4), BF16),
            shape((16, points // 4), BF16),
            shape((shared, 64, 128), BF16),
            shape((shared, 64, 128), BF16),
            shape((2, chips, tops // 2, 64, 128), BF16),
        ),
        in_specs=[smem(), smem()] + [vmem()] * 3 + [hbm()] * 3,
        out_specs=(vmem(),) * 11,
        scratch_shapes=[
            pltpu.VMEM((points, 128), F32),
            pltpu.VMEM((points, 128), F32),
            pltpu.VMEM(leaf_basis.shape, BF16),
            pltpu.VMEM(transfer_low.shape, BF16),
            pltpu.VMEM(transfer_top.shape, BF16),
            dma((3,)),
            dma((2 * CHUNKS + 4,)),
            dma((2 * CHUNKS + 4,)),
            dma((chips,)),
            dma((chips,)),
            dma,
            dma,
        ],
        compiler_params=pltpu.CompilerParams(
            vmem_limit_bytes=VMEM_BYTES, collective_id=0, has_side_effects=True
        ),
        cost_estimate=pl.CostEstimate(flops=10**9, bytes_accessed=2 * 10**7, transcendentals=0),
        name="prep",
    )(order, near_count, coords, probes, near_list, leaf_basis, transfer_low, transfer_top)
    tree, cells, coef, counts, left, right = exchanged[:6]
    cells_left, cells_right, coef_left, coef_right, gathered = exchanged[6:]

    return pl.pallas_call(
        apply_kernel,
        out_shape=shape((64, points), F32),
        in_specs=[smem()] * 5 + [vmem()] * 13 + [hbm()] * 3,
        out_specs=vmem(),
        scratch_shapes=[
            pltpu.VMEM((leaves, FEATURES, LEAF), BF16),
            pltpu.VMEM((3 * leaves, LEAF, FEATURES), BF16),
            pltpu.VMEM((3 * leaves, 64, LEAF), BF16),
            pltpu.SMEM((leaves * (2 * leaves + 1) + GROUP,), jnp.int32),
            pltpu.VMEM((leaves, 64, LEAF), F32),
            pltpu.VMEM((3 * leaves, 64, 128), BF16),
            pltpu.VMEM((3 * mids, 64, 128), BF16),
            pltpu.VMEM((tops * count, 64, 128), BF16),
            pltpu.VMEM(coupling_leaf.shape, BF16),
            pltpu.VMEM(coupling_mid.shape, BF16),
            pltpu.VMEM(coupling_top.shape, BF16),
            pltpu.VMEM((leaves + mids + tops, 64, 64), F32),
            pltpu.VMEM((points, 128), F32),
            pltpu.VMEM((points, 128), F32),
            pltpu.SemaphoreType.DMA((3,)),
        ],
        compiler_params=pltpu.CompilerParams(vmem_limit_bytes=VMEM_BYTES),
        cost_estimate=pl.CostEstimate(
            flops=2 * 10**10, bytes_accessed=2 * 10**7, transcendentals=10**7
        ),
        name="apply",
    )(
        counts, order, far_leaf, far_mid, far_top,
        tree, left, right, cells, cells_left, cells_right, coef, coef_left, coef_right, gathered,
        leaf_basis, transfer_low, transfer_top, coupling_leaf, coupling_mid, coupling_top,
    )


def solution(mesh):
    both = ("groups", "col")
    return jax.shard_map(
        per_device,
        mesh=mesh,
        in_specs=(
            P(None, both),
            P(None, both),
            P(both),
            P(both, None),
            P(both),
            P(both, None, None),
            P(both, None, None),
            P(both, None, None),
            P(both, None, None, None),
            P(both, None, None, None),
            P(both, None, None, None),
            P(both, None),
            P(both, None),
            P(both, None),
        ),
        out_specs=P(None, both),
        check_vma=False,
    )
```

profile of v0, /device:TPU:9, one launch (start us, length us, event | category | flops | bytes accessed | tf_op | source)
XLA Modules:
  0.0 65.4 jit_solution(9055167170533339502)
XLA Ops:
  0.0 27.5 %prep.1 = (bf16[64,4096]{1,0:T(8,128)(2,1)}, bf16[16,1024]{1,0:T(8,128)(2,1)}, bf16[12,64,128]{2,1,0:T(8,128)(2,1)}, s32[16,128]{1,0:T(8,128)}, bf16[64,4096]{1,...) custom-call(s32[4096]{0:T(1024)} %order.3, ...), custom_call_target="tpu_custom_call" | custom-call | flops 1000000000 | bytes 20000000 | tf_op jit(solution)/shard_map/prep/pallas_call | solution.py:438
  27.5 37.9 %apply.1 = f32[64,4096]{1,0:T(8,128)} custom-call(s32[16,128]{1,0:T(8,128)} %get-tuple-element.16.counts, s32[4096]{0:T(1024)} %order.3, s32[16,16]{1,0:T(8,128)} %far_leaf.1, s32[8,16]{1,0:T(8,128)} %far_mid.1, s32[4,16]{1,0:T(4,128)} %far_top.1, bf16[64,4096]{1,0:T(8,128)(2,1)} %get-tuple-element.17.own, bf16[64,4096]{1,0:T(8,128)(2,1)} %get-tuple-element.18.left, ...), custom_call_target="tpu_custom_call" | custom-call | flops 20000000000 | bytes 20000000 | tf_op jit(solution)/shard_map/apply/pallas_call | solution.py:478
where the time goes:
time: 65.5 us; the launch traced here: 65.4 us
  Pallas kernels  65.4 us (100%)
    pallas_call x1, Pallas kernels, per_device(): pl.pallas_call(apply_kernel, out_shape=shape((64, points), F32), in_specs...  37.9 us
    pallas_call x1, Pallas kernels, per_device(): pl.pallas_call(prep_kernel, out_shape=(shape((64, points), BF16), shape((...  27.5 us

commit v1 on v0

--- a/solution.py
+++ b/solution.py
@@ -10,6 +10,7 @@
 LENGTH_SCALE = 1.0
 GROUP = 16
 CHUNKS = 4
+STEADY = 6
 FEATURES = 48
 BF16 = jnp.bfloat16
 F32 = jnp.float32
@@ -26,6 +27,12 @@
     return lax.dot_general(a, b, NT, preferred_element_type=F32)
 
 
+def near_tile(source, target):
+    squared = jnp.maximum(dot(source, target), 1e-30)
+    distance = squared * lax.rsqrt(squared)
+    return jnp.exp(distance * (-1.0 / LENGTH_SCALE)).astype(BF16)
+
+
 def within(position, points):
     if points & (points - 1) == 0:
         return position & (points - 1)
@@ -35,8 +42,8 @@
 def prep_kernel(
     order, near_count, coords, probes, near_list, basis_hbm, low_hbm, top_hbm,
     points_out, cells_out, coef_out, counts_out,
-    left, right, cells_left, cells_right, coef_left, coef_right, tops,
-    rows_in, rows_out, basis, low, top,
+    left, right, cells_left, cells_right, coef_left, coef_right, tops, field_out,
+    rows_in, rows_out, basis, low, top, targets, sources, values,
     load_sems, send_sems, recv_sems, top_send, top_recv, pair_send, pair_recv,
 ):
     points = coords.shape[1]
@@ -192,7 +199,26 @@
         named = near_list[:, k : k + 1] - start
         total = total + jnp.where((named == lane) & (live > k), 1, 0)
     inside = (lane + start >= 0) & (lane + start < spans * leaves)
-    counts_out[...] = jnp.where(inside, total, 0)
+    total = jnp.where(inside, total, 0)
+    counts_out[...] = total
+
+    fill_targets(cells_out, targets)
+    fill_sources(points_out, cells_out, sources, values, 0)
+    field_out[...] = jnp.zeros_like(field_out)
+
+    def steady(lo, hi):
+        @pl.loop(lo, hi)
+        def _(d):
+            chosen = lane == leaves + (row + d) % leaves
+            weight = jnp.sum(jnp.where(chosen, total, 0).astype(F32), axis=1, keepdims=True)
+            weight = weight * AMPLITUDE
+            slots = [(i + d) % leaves for i in range(leaves)]
+            tiles = [near_tile(sources[slots[i]], targets[i]) for i in range(leaves)]
+            sums = [dot(values[slots[i]], tiles[i]) * weight[i : i + 1] for i in range(leaves)]
+            for i in range(leaves):
+                field_out[i] += sums[i]
+
+    steady(0, STEADY // 2)
 
     @pl.loop(1, chips)
     def _(j):
@@ -207,6 +233,7 @@
         device_id_type=MESH,
     )
     pair.start()
+    steady(STEADY // 2, STEADY)
 
     @pl.when(jnp.logical_not(is_last))
     def _():
@@ -261,6 +288,8 @@
     def one(i, position):
         for j in range(2 * leaves + 1):
             count = counts[i, i + j]
+            if (j - leaves) % leaves < STEADY:
+                count = jnp.where((i + j >= leaves) & (i + j < 2 * leaves), 0, count)
             listed[position] = count * 4096 + (i * 64 + i + j)
             position = position + jnp.minimum(count, 1)
         return position
@@ -278,11 +307,7 @@
         slots = [pair & 63 for pair in pairs]
         owners = [(pair >> 6) & 63 for pair in pairs]
         weights = [(pair >> 12).astype(F32) * AMPLITUDE for pair in pairs]
-        tiles = []
-        for u in range(GROUP):
-            squared = jnp.maximum(dot(sources[slots[u]], targets[owners[u]]), 1e-30)
-            distance = squared * lax.rsqrt(squared)
-            tiles.append(jnp.exp(distance * (-1.0 / LENGTH_SCALE)).astype(BF16))
+        tiles = [near_tile(sources[slots[u]], targets[owners[u]]) for u in range(GROUP)]
         sums = [dot(values[slots[u]], tiles[u]) * weights[u] for u in range(GROUP)]
         for u in range(GROUP):
             field[owners[u]] += sums[u]
@@ -291,7 +316,7 @@
 def apply_kernel(
     counts, order, far_leaf, far_mid, far_top,
     own, left, right, cells_own, cells_left, cells_right,
-    coef_own, coef_left, coef_right, tops,
+    coef_own, coef_left, coef_right, tops, field_in,
     basis, low, top, couple_leaf_hbm, couple_mid_hbm, couple_top_hbm,
     out,
     targets, sources, values, listed, field,
@@ -314,7 +339,7 @@
     fill_sources(left, cells_left, sources, values, 0)
     fill_sources(own, cells_own, sources, values, leaves)
     fill_sources(right, cells_right, sources, values, 2 * leaves)
-    field[...] = jnp.zeros_like(field)
+    field[...] = field_in[...]
     groups = list_pairs(counts, listed, leaves)
     add_pairs(listed, groups, targets, sources, values, field)
 
@@ -449,15 +474,19 @@
             shape((shared, 64, 128), BF16),
             shape((shared, 64, 128), BF16),
             shape((2, chips, tops // 2, 64, 128), BF16),
+            shape((leaves, 64, LEAF), F32),
         ),
         in_specs=[smem(), smem()] + [vmem()] * 3 + [hbm()] * 3,
-        out_specs=(vmem(),) * 11,
+        out_specs=(vmem(),) * 12,
         scratch_shapes=[
             pltpu.VMEM((points, 128), F32),
             pltpu.VMEM((points, 128), F32),
             pltpu.VMEM(leaf_basis.shape, BF16),
             pltpu.VMEM(transfer_low.shape, BF16),
             pltpu.VMEM(transfer_top.shape, BF16),
+            pltpu.VMEM((leaves, FEATURES, LEAF), BF16),
+            pltpu.VMEM((leaves, LEAF, FEATURES), BF16),
+            pltpu.VMEM((leaves, 64, LEAF), BF16),
             dma((3,)),
             dma((2 * CHUNKS + 4,)),
             dma((2 * CHUNKS + 4,)),
@@ -473,12 +502,12 @@
         name="prep",
     )(order, near_count, coords, probes, near_list, leaf_basis, transfer_low, transfer_top)
     tree, cells, coef, counts, left, right = exchanged[:6]
-    cells_left, cells_right, coef_left, coef_right, gathered = exchanged[6:]
+    cells_left, cells_right, coef_left, coef_right, gathered, field = exchanged[6:]
 
     return pl.pallas_call(
         apply_kernel,
         out_shape=shape((64, points), F32),
-        in_specs=[smem()] * 5 + [vmem()] * 13 + [hbm()] * 3,
+        in_specs=[smem()] * 5 + [vmem()] * 14 + [hbm()] * 3,
         out_specs=vmem(),
         scratch_shapes=[
             pltpu.VMEM((leaves, FEATURES, LEAF), BF16),
@@ -504,7 +533,7 @@
         name="apply",
     )(
         counts, order, far_leaf, far_mid, far_top,
-        tree, left, right, cells, cells_left, cells_right, coef, coef_left, coef_right, gathered,
+        tree, left, right, cells, cells_left, cells_right, coef, coef_left, coef_right, gathered, field,
         leaf_basis, transfer_low, transfer_top, coupling_leaf, coupling_mid, coupling_top,
     )
 

time: 65.5 us -> 64.7 us (0.988)
  the two profiles are of different devices: /device:TPU:9 before, /device:TPU:12 now
where the time goes in v1:
time: 64.7 us; the launch traced here: 63.8 us
  Pallas kernels  63.8 us (99%)
    pallas_call x1, Pallas kernels, per_device(): pl.pallas_call(apply_kernel, out_shape=shape((64, points), F32), in_specs...  35.1 us
    pallas_call x1, Pallas kernels, per_device(): pl.pallas_call(prep_kernel, out_shape=(shape((64, points), BF16), shape((...  28.7 us

profile of v1, /device:TPU:12, one launch (start us, length us, event | category | flops | bytes accessed | tf_op | source)
XLA Modules:
  0.0 63.8 jit_solution(12251029105458144570)
XLA Ops:
  0.0 28.7 %prep.1 = (bf16[64,4096]{1,0:T(8,128)(2,1)}, bf16[16,1024]{1,0:T(8,128)(2,1)}, bf16[12,64,128]{2,1,0:T(8,128)(2,1)}, s32[16,128]{1,0:T(8,128)}, bf16[64,4096]{1,...) custom-call(s32[4096]{0:T(1024)} %order.3, ...), custom_call_target="tpu_custom_call" | custom-call | flops 1000000000 | bytes 20000000 | tf_op jit(solution)/shard_map/prep/pallas_call | solution.py:463
  28.7 35.1 %apply.1 = f32[64,4096]{1,0:T(8,128)} custom-call(s32[16,128]{1,0:T(8,128)} %get-tuple-element.17.counts, s32[4096]{0:T(1024)} %order.3, s32[16,16]{1,0:T(8,128)} %far_leaf.1, s32[8,16]{1,0:T(8,128)} %far_mid.1, s32[4,16]{1,0:T(4,128)} %far_top.1, bf16[64,4096]{1,0:T(8,128)(2,1)} %get-tuple-element.18.own, bf16[64,4096]{1,0:T(8,128)(2,1)} %get-tuple-element.19.left, ...), custom_call_target="tpu_custom_call" | custom-call | flops 20000000000 | bytes 20000000 | tf_op jit(solution)/shard_map/apply/pallas_call | solution.py:507
